TPU v7x, 128 devices: a whole 4x4x4 slice. The times are simulated.
128 devices in a mesh: ctx: 32 (over y, x, core), rows: 4 (over z).
Axes of the slice: x: 4, y: 4, z: 4, core: 2. Of those that a mesh axis runs over, the one named last changes fastest.
Arguments:
- queries: bfloat16 [64, 8192], P('rows', 'ctx'), may hold values from -200 to 200
- keys: bfloat16 [64, 8192, 1024], P('rows', 'ctx'), may hold values from -6 to 6
- values: bfloat16 [64, 8192, 1024], P('rows', 'ctx'), may hold values from -6 to 6
- codes: int32 [64, 8192, 128], P('rows', 'ctx'), may hold values from 0 to 255
- codebook: bfloat16 [8, 16, 256, 8], replicated, may hold values from -15 to 15
- lengths: int32 [64], P('rows'), may hold values from 1024 to 8192, as said below
- blocks: int32 [64, 8, 16], P('rows'), may hold values from 0 to 127, as said below
Outputs:
- attended: bfloat16 [64, 8192], P('rows', 'ctx')
- approx_mass: float32 [64, 64], P('rows', 'ctx')
Inputs may be any that keep to these rules, and one draw needn't show every extreme that they name: `lengths`: row 0 has the whole context. Each row and key-value head names 16 different blocks, each holding some position below the row's length.
All inputs are finite; a program needn't handle non-finite values.
Results may differ from a plain program's by a relative error of at most 0.02.
Values may be sent and summed in bfloat16 or wider, within the bound.
A program may use at most 128 MiB of HBM per device.

v0:
```python
import jax
import jax.numpy as jnp
from jax import lax
from jax.sharding import PartitionSpec as P

H = 64
KVH = 8
HD = 128
M = 16
CODES = 256
BLK = 64


NEGATIVE = -1e30


def combined_all(part, axis, combine):
    gathered = jax.tree.map(lambda a: lax.all_gather(a, axis), part)

    def take(source):
        return jax.tree.map(lambda a: lax.dynamic_index_in_dim(a, source, 0, False), gathered)

    return lax.fori_loop(
        1, lax.axis_size(axis), lambda source, state: combine(state, take(source)), take(0)
    )


def combine_pair(earlier, later):
    peak = jnp.maximum(earlier[0], later[0])
    return (peak, earlier[1] * jnp.exp(earlier[0] - peak) + later[1] * jnp.exp(later[0] - peak))


def combine_three(earlier, later):
    peak = jnp.maximum(earlier[0], later[0])
    factor_one = jnp.exp(earlier[0] - peak)
    factor_two = jnp.exp(later[0] - peak)
    return (
        peak,
        earlier[1] * factor_one + later[1] * factor_two,
        earlier[2] * factor_one[..., None] + later[2] * factor_two[..., None],
    )


def row_scores(row_items):
    code_rows, lookup_row = row_items
    one_hot = (code_rows[..., None] == jnp.arange(CODES, dtype=jnp.int32)).astype(jnp.bfloat16)
    return jnp.einsum("tgmc,gjmc->gjt", one_hot, lookup_row, preferred_element_type=jnp.float32)


def body(queries, keys, values, codes, codebook, lengths, blocks):
    score_scale = HD ** (-0.5)
    groups = H // KVH
    query_all = lax.all_gather(queries, "ctx", axis=1, tiled=True)
    row_count = query_all.shape[0]
    local_len = keys.shape[1]
    split_query = query_all.reshape(row_count, KVH, groups, M, HD // M)
    lookup = (
        jnp.einsum("rgjms,gmcs->rgjmc", split_query, codebook, preferred_element_type=jnp.float32)
        * score_scale
    ).astype(jnp.bfloat16)
    approx = lax.map(row_scores, (codes.reshape(row_count, local_len, KVH, M), lookup))
    position = lax.axis_index("ctx") * local_len + jnp.arange(local_len, dtype=jnp.int32)
    inside = position[None, :] < lengths[:, None]
    inside_wide = inside[:, None, None, :]
    approx_peak = jnp.max(jnp.where(inside_wide, approx, NEGATIVE), axis=-1)
    approx_total = jnp.sum(
        jnp.where(inside_wide, jnp.exp(approx - approx_peak[..., None]), 0.0), axis=-1
    )
    key_heads = keys.reshape(row_count, local_len, KVH, HD)
    value_heads = values.reshape(row_count, local_len, KVH, HD)
    query_heads = query_all.reshape(row_count, KVH, groups, HD)
    scores = (
        jnp.einsum("rgjd,rtgd->rgjt", query_heads, key_heads, preferred_element_type=jnp.float32)
        * score_scale
    )
    block_of = position // BLK
    chosen_mask = jnp.any(blocks[:, :, :, None] == block_of[None, None, None, :], axis=2)
    used = (chosen_mask & inside[:, None, :])[:, :, None, :]
    attn_peak = jnp.max(jnp.where(used, scores, NEGATIVE), axis=-1)
    weights = jnp.where(used, jnp.exp(scores - attn_peak[..., None]), 0.0)
    attn_total = jnp.sum(weights, axis=-1)
    weighted = jnp.einsum(
        "rgjt,rtgd->rgjd",
        weights.astype(jnp.bfloat16),
        value_heads,
        preferred_element_type=jnp.float32,
    )
    head_share = H // lax.axis_size("ctx")
    approx_peak, approx_total = combined_all((approx_peak, approx_total), "ctx", combine_pair)
    attn_peak, attn_total, weighted = combined_all(
        (attn_peak, attn_total, weighted), "ctx", combine_three
    )
    log_mass = (approx_peak + jnp.log(approx_total)).reshape(row_count, H)
    attended = (weighted / attn_total[..., None]).reshape(row_count, H * HD)
    mass_part = lax.dynamic_slice_in_dim(
        log_mass, lax.axis_index("ctx") * head_share, head_share, 1
    )
    attended_part = lax.dynamic_slice_in_dim(
        attended, lax.axis_index("ctx") * head_share * HD, head_share * HD, 1
    )
    return (attended_part.astype(jnp.bfloat16), mass_part)


def solution(mesh):
    placed = (
        P("rows", "ctx"),
        P("rows", "ctx", None),
        P("rows", "ctx", None),
        P("rows", "ctx", None),
        P(),
        P("rows"),
        P("rows", None, None),
    )
    return jax.shard_map(
        body,
        mesh=mesh,
        in_specs=placed,
        out_specs=(P("rows", "ctx"), P("rows", "ctx")),
        check_vma=False,
    )
```

profile of v0, /device:TPU:1, one launch (start us, length us, event | category | flops | bytes accessed | tf_op | source)
XLA Modules:
  0.0 501.9 jit_solution(2344543356521164878)
XLA Ops:
  8.1 27.7 %all_gather.33 = bf16[16,8192]{0,1:T(8,128)(2,1)S(1)} all-gather(bf16[16,256]{0,1:T(8,128)(2,1)S(1)} %copy.58), channel_id=1, replica_groups=mesh['ctx'=32,'rows'=4] {'ctx'}, dimensions={1}, use_global_device_ids=true | all-gather | bytes 270336 | tf_op jit(solution)/shard_map/all_gather | solution.py:53
  65.3 212.0 %while.50 = (s32[]{:T(128)}, f32[16,8,8,256]{3,2,1,0:T(8,128)S(1)}, bf16[16,8,8,16,256]{4,2,3,1,0:T(8,128)(2,1)}, s32[16,256,8,16]{1,3,2,0:T(8,128)}) while((s32[]{:T(128)}, f32[16,8,8,256]{3,2,1,0:T(8,128)S(1)}, bf16[16,8,8,16,256]{4,2,3,1,0:T(8,128)(2,1)}, s32[16,256,8,16]{1,3,2,0:T(8,128)}) %tuple.127), condition=%wide.region_6.7_spmd.clone, body=%wide.region_5.6_spmd.sunk.clone | while | flops 142606336 | bytes 2031681 | solution.py:61
  67.3 11.2 %fusion.56 = f32[16,8,8,256]{3,2,1,0:T(8,128)S(1)} fusion(f32[16,8,8,256]{3,2,1,0:T(8,128)S(1)} %get-tuple-element.618, s32[]{:T(128)} %get-tuple-element.617, s32[256,8,16]{0,2,1:T(8,128)S(1)} %dynamic-slice_bitcast_fusion.3, bf16[8,8,16,256]{3,1,2,0:T(8,128)(2,1)S(1)} %fusion.55), kind=kOutput, calls=%fused_computation.12.clone.3.clone | convolution fusion | flops 142606336 | bytes 720900 | tf_op jit(solution)/shard_map/while/body/eval_jaxpr/tgmc,gjmc->gjt/dot_general | solution.py:47
  80.5 11.2 %fusion.56 = f32[16,8,8,256]{3,2,1,0:T(8,128)S(1)} fusion(f32[16,8,8,256]{3,2,1,0:T(8,128)S(1)} %get-tuple-element.618, s32[]{:T(128)} %get-tuple-element.617, s32[256,8,16]{0,2,1:T(8,128)S(1)} %dynamic-slice_bitcast_fusion.3, bf16[8,8,16,256]{3,1,2,0:T(8,128)(2,1)S(1)} %fusion.55), kind=kOutput, calls=%fused_computation.12.clone.3.clone | convolution fusion | flops 142606336 | bytes 720900 | tf_op jit(solution)/shard_map/while/body/eval_jaxpr/tgmc,gjmc->gjt/dot_general | solution.py:47
  93.8 11.2 %fusion.56 = f32[16,8,8,256]{3,2,1,0:T(8,128)S(1)} fusion(f32[16,8,8,256]{3,2,1,0:T(8,128)S(1)} %get-tuple-element.618, s32[]{:T(128)} %get-tuple-element.617, s32[256,8,16]{0,2,1:T(8,128)S(1)} %dynamic-slice_bitcast_fusion.3, bf16[8,8,16,256]{3,1,2,0:T(8,128)(2,1)S(1)} %fusion.55), kind=kOutput, calls=%fused_computation.12.clone.3.clone | convolution fusion | flops 142606336 | bytes 720900 | tf_op jit(solution)/shard_map/while/body/eval_jaxpr/tgmc,gjmc->gjt/dot_general | solution.py:47
  107.1 11.2 %fusion.56 = f32[16,8,8,256]{3,2,1,0:T(8,128)S(1)} fusion(f32[16,8,8,256]{3,2,1,0:T(8,128)S(1)} %get-tuple-element.618, s32[]{:T(128)} %get-tuple-element.617, s32[256,8,16]{0,2,1:T(8,128)S(1)} %dynamic-slice_bitcast_fusion.3, bf16[8,8,16,256]{3,1,2,0:T(8,128)(2,1)S(1)} %fusion.55), kind=kOutput, calls=%fused_computation.12.clone.3.clone | convolution fusion | flops 142606336 | bytes 720900 | tf_op jit(solution)/shard_map/while/body/eval_jaxpr/tgmc,gjmc->gjt/dot_general | solution.py:47
  120.3 11.2 %fusion.56 = f32[16,8,8,256]{3,2,1,0:T(8,128)S(1)} fusion(f32[16,8,8,256]{3,2,1,0:T(8,128)S(1)} %get-tuple-element.618, s32[]{:T(128)} %get-tuple-element.617, s32[256,8,16]{0,2,1:T(8,128)S(1)} %dynamic-slice_bitcast_fusion.3, bf16[8,8,16,256]{3,1,2,0:T(8,128)(2,1)S(1)} %fusion.55), kind=kOutput, calls=%fused_computation.12.clone.3.clone | convolution fusion | flops 142606336 | bytes 720900 | tf_op jit(solution)/shard_map/while/body/eval_jaxpr/tgmc,gjmc->gjt/dot_general | solution.py:47
  133.6 11.2 %fusion.56 = f32[16,8,8,256]{3,2,1,0:T(8,128)S(1)} fusion(f32[16,8,8,256]{3,2,1,0:T(8,128)S(1)} %get-tuple-element.618, s32[]{:T(128)} %get-tuple-element.617, s32[256,8,16]{0,2,1:T(8,128)S(1)} %dynamic-slice_bitcast_fusion.3, bf16[8,8,16,256]{3,1,2,0:T(8,128)(2,1)S(1)} %fusion.55), kind=kOutput, calls=%fused_computation.12.clone.3.clone | convolution fusion | flops 142606336 | bytes 720900 | tf_op jit(solution)/shard_map/while/body/eval_jaxpr/tgmc,gjmc->gjt/dot_general | solution.py:47
  146.8 11.2 %fusion.56 = f32[16,8,8,256]{3,2,1,0:T(8,128)S(1)} fusion(f32[16,8,8,256]{3,2,1,0:T(8,128)S(1)} %get-tuple-element.618, s32[]{:T(128)} %get-tuple-element.617, s32[256,8,16]{0,2,1:T(8,128)S(1)} %dynamic-slice_bitcast_fusion.3, bf16[8,8,16,256]{3,1,2,0:T(8,128)(2,1)S(1)} %fusion.55), kind=kOutput, calls=%fused_computation.12.clone.3.clone | convolution fusion | flops 142606336 | bytes 720900 | tf_op jit(solution)/shard_map/while/body/eval_jaxpr/tgmc,gjmc->gjt/dot_general | solution.py:47
  160.1 11.2 %fusion.56 = f32[16,8,8,256]{3,2,1,0:T(8,128)S(1)} fusion(f32[16,8,8,256]{3,2,1,0:T(8,128)S(1)} %get-tuple-element.618, s32[]{:T(128)} %get-tuple-element.617, s32[256,8,16]{0,2,1:T(8,128)S(1)} %dynamic-slice_bitcast_fusion.3, bf16[8,8,16,256]{3,1,2,0:T(8,128)(2,1)S(1)} %fusion.55), kind=kOutput, calls=%fused_computation.12.clone.3.clone | convolution fusion | flops 142606336 | bytes 720900 | tf_op jit(solution)/shard_map/while/body/eval_jaxpr/tgmc,gjmc->gjt/dot_general | solution.py:47
  173.3 11.2 %fusion.56 = f32[16,8,8,256]{3,2,1,0:T(8,128)S(1)} fusion(f32[16,8,8,256]{3,2,1,0:T(8,128)S(1)} %get-tuple-element.618, s32[]{:T(128)} %get-tuple-element.617, s32[256,8,16]{0,2,1:T(8,128)S(1)} %dynamic-slice_bitcast_fusion.3, bf16[8,8,16,256]{3,1,2,0:T(8,128)(2,1)S(1)} %fusion.55), kind=kOutput, calls=%fused_computation.12.clone.3.clone | convolution fusion | flops 142606336 | bytes 720900 | tf_op jit(solution)/shard_map/while/body/eval_jaxpr/tgmc,gjmc->gjt/dot_general | solution.py:47
  186.6 11.2 %fusion.56 = f32[16,8,8,256]{3,2,1,0:T(8,128)S(1)} fusion(f32[16,8,8,256]{3,2,1,0:T(8,128)S(1)} %get-tuple-element.618, s32[]{:T(128)} %get-tuple-element.617, s32[256,8,16]{0,2,1:T(8,128)S(1)} %dynamic-slice_bitcast_fusion.3, bf16[8,8,16,256]{3,1,2,0:T(8,128)(2,1)S(1)} %fusion.55), kind=kOutput, calls=%fused_computation.12.clone.3.clone | convolution fusion | flops 142606336 | bytes 720900 | tf_op jit(solution)/shard_map/while/body/eval_jaxpr/tgmc,gjmc->gjt/dot_general | solution.py:47
  199.8 11.2 %fusion.56 = f32[16,8,8,256]{3,2,1,0:T(8,128)S(1)} fusion(f32[16,8,8,256]{3,2,1,0:T(8,128)S(1)} %get-tuple-element.618, s32[]{:T(128)} %get-tuple-element.617, s32[256,8,16]{0,2,1:T(8,128)S(1)} %dynamic-slice_bitcast_fusion.3, bf16[8,8,16,256]{3,1,2,0:T(8,128)(2,1)S(1)} %fusion.55), kind=kOutput, calls=%fused_computation.12.clone.3.clone | convolution fusion | flops 142606336 | bytes 720900 | tf_op jit(solution)/shard_map/while/body/eval_jaxpr/tgmc,gjmc->gjt/dot_general | solution.py:47
  213.0 11.2 %fusion.56 = f32[16,8,8,256]{3,2,1,0:T(8,128)S(1)} fusion(f32[16,8,8,256]{3,2,1,0:T(8,128)S(1)} %get-tuple-element.618, s32[]{:T(128)} %get-tuple-element.617, s32[256,8,16]{0,2,1:T(8,128)S(1)} %dynamic-slice_bitcast_fusion.3, bf16[8,8,16,256]{3,1,2,0:T(8,128)(2,1)S(1)} %fusion.55), kind=kOutput, calls=%fused_computation.12.clone.3.clone | convolution fusion | flops 142606336 | bytes 720900 | tf_op jit(solution)/shard_map/while/body/eval_jaxpr/tgmc,gjmc->gjt/dot_general | solution.py:47
  226.3 11.2 %fusion.56 = f32[16,8,8,256]{3,2,1,0:T(8,128)S(1)} fusion(f32[16,8,8,256]{3,2,1,0:T(8,128)S(1)} %get-tuple-element.618, s32[]{:T(128)} %get-tuple-element.617, s32[256,8,16]{0,2,1:T(8,128)S(1)} %dynamic-slice_bitcast_fusion.3, bf16[8,8,16,256]{3,1,2,0:T(8,128)(2,1)S(1)} %fusion.55), kind=kOutput, calls=%fused_computation.12.clone.3.clone | convolution fusion | flops 142606336 | bytes 720900 | tf_op jit(solution)/shard_map/while/body/eval_jaxpr/tgmc,gjmc->gjt/dot_general | solution.py:47
  239.5 11.2 %fusion.56 = f32[16,8,8,256]{3,2,1,0:T(8,128)S(1)} fusion(f32[16,8,8,256]{3,2,1,0:T(8,128)S(1)} %get-tuple-element.618, s32[]{:T(128)} %get-tuple-element.617, s32[256,8,16]{0,2,1:T(8,128)S(1)} %dynamic-slice_bitcast_fusion.3, bf16[8,8,16,256]{3,1,2,0:T(8,128)(2,1)S(1)} %fusion.55), kind=kOutput, calls=%fused_computation.12.clone.3.clone | convolution fusion | flops 142606336 | bytes 720900 | tf_op jit(solution)/shard_map/while/body/eval_jaxpr/tgmc,gjmc->gjt/dot_general | solution.py:47
  252.8 11.2 %fusion.56 = f32[16,8,8,256]{3,2,1,0:T(8,128)S(1)} fusion(f32[16,8,8,256]{3,2,1,0:T(8,128)S(1)} %get-tuple-element.618, s32[]{:T(128)} %get-tuple-element.617, s32[256,8,16]{0,2,1:T(8,128)S(1)} %dynamic-slice_bitcast_fusion.3, bf16[8,8,16,256]{3,1,2,0:T(8,128)(2,1)S(1)} %fusion.55), kind=kOutput, calls=%fused_computation.12.clone.3.clone | convolution fusion | flops 142606336 | bytes 720900 | tf_op jit(solution)/shard_map/while/body/eval_jaxpr/tgmc,gjmc->gjt/dot_general | solution.py:47
  266.0 11.2 %fusion.56 = f32[16,8,8,256]{3,2,1,0:T(8,128)S(1)} fusion(f32[16,8,8,256]{3,2,1,0:T(8,128)S(1)} %get-tuple-element.618, s32[]{:T(128)} %get-tuple-element.617, s32[256,8,16]{0,2,1:T(8,128)S(1)} %dynamic-slice_bitcast_fusion.3, bf16[8,8,16,256]{3,1,2,0:T(8,128)(2,1)S(1)} %fusion.55), kind=kOutput, calls=%fused_computation.12.clone.3.clone | convolution fusion | flops 142606336 | bytes 720900 | tf_op jit(solution)/shard_map/while/body/eval_jaxpr/tgmc,gjmc->gjt/dot_general | solution.py:47
  277.9 25.7 %all-gather.4 = f32[512,8,8]{2,1,0:T(8,128)S(1)} all-gather(f32[16,8,8]{2,1,0:T(8,128)S(1)} %select_reduce_fusion), channel_id=6, replica_groups=mesh['ctx'=32,'rows'=4] {'ctx'}, dimensions={0}, use_global_device_ids=true | all-gather | bytes 135168 | tf_op jit(solution)/shard_map/all_gather | solution.py:18
  308.3 23.9 %all-gather.3 = f32[512,8,8]{2,1,0:T(8,128)S(1)} all-gather(f32[16,8,8]{2,1,0:T(8,128)S(1)} %select_reduce_fusion.1), channel_id=5, replica_groups=mesh['ctx'=32,'rows'=4] {'ctx'}, dimensions={0}, use_global_device_ids=true | all-gather | bytes 135168 | tf_op jit(solution)/shard_map/all_gather | solution.py:18
  337.2 25.4 %all-gather.1 = f32[512,8,8]{2,1,0:T(8,128)S(1)} all-gather(f32[16,8,8]{2,1,0:T(8,128)S(1)} %fusion.24), channel_id=3, replica_groups=mesh['ctx'=32,'rows'=4] {'ctx'}, dimensions={0}, use_global_device_ids=true | all-gather | bytes 135168 | tf_op jit(solution)/shard_map/all_gather | solution.py:18
  364.3 23.9 %all-gather = f32[512,8,8]{2,1,0:T(8,128)S(1)} all-gather(f32[16,8,8]{2,1,0:T(8,128)S(1)} %get-tuple-element.429), channel_id=2, replica_groups=mesh['ctx'=32,'rows'=4] {'ctx'}, dimensions={0}, use_global_device_ids=true | all-gather | bytes 135168 | tf_op jit(solution)/shard_map/all_gather | solution.py:18
  389.9 25.9 %while.51 = (s32[]{:T(128)}, f32[16,8,8]{0,2,1:T(8,128)S(1)}, f32[16,8,8]{0,2,1:T(8,128)S(1)}, f32[32,16,8,8]{1,3,2,0:T(8,128)}, f32[32,16,8,8]{1,3,2,0:T(8,128)}) while((s32[]{:T(128)}, f32[16,8,8]{0,2,1:T(8,128)S(1)}, f32[16,8,8]{0,2,1:T(8,128)S(1)}, f32[32,16,8,8]{1,3,2,0:T(8,128)}, f32[32,16,8,8]{1,3,2,0:T(8,128)}) %tuple.121), condition=%wide.region_10.11_spmd.clone, body=%wide.region_9.10_spmd.sunk.clone | while | flops 6149 | bytes 24683 | solution.py:23
  417.5 76.5 %while.49 = (s32[]{:T(128)}, f32[16,8,8]{0,2,1:T(8,128)S(1)}, f32[16,8,8]{0,2,1:T(8,128)S(1)}, f32[16,8,8,128]{3,2,1,0:T(8,128)S(1)}, f32[32,16,8,8]{1,3,2,0:T(8...) while((s32[]{:T(128)}, f32[16,8,8]{0,2,1:T(8,128)S(1)}, ...), condition=%wide.region_4.5_spmd.clone, body=%wide.region_3.4_spmd.sunk.clone | while | flops 399365 | bytes 1630335 | solution.py:23
  (240 shorter events, 179.4 us)
Async XLA Ops:
  7.2 40.9 %copy-start = (bf16[8,16,256,8]{2,3,1,0:T(8,128)(2,1)S(1)}, bf16[8,16,256,8]{2,3,1,0:T(8,128)(2,1)}, u32[]{:S(2)}) copy-start(bf16[8,16,256,8]{2,3,1,0:T(8,128)(2,1)} %param.17) | copy-start | bytes 1572868
  7.2 409.2 %all-gather.7.cloned.1.call-start = ((), (), s32[]{:S(2)}) async-start(), calls=%async_computation | async-start | bytes 17301504 | tf_op jit(solution)/shard_map/all_gather | solution.py:18
  36.7 9.2 %copy-start.6 = (bf16[16,256,1024]{2,1,0:T(8,128)(2,1)S(1)}, bf16[16,256,1024]{2,1,0:T(8,128)(2,1)}, u32[]{:S(2)}) copy-start(bf16[16,256,1024]{2,1,0:T(8,128)(2,1)} %param.15) | copy-start | bytes 25165828
  45.0 1.0 copy-start.2
  52.7 12.6 %copy-start.7 = (f32[16,8,8,256]{3,2,1,0:T(8,128)S(1)}, f32[16,8,8,256]{3,2,1,0:T(8,128)}, u32[]{:S(2)}) copy-start(f32[16,8,8,256]{3,2,1,0:T(8,128)} %custom-call) | copy-start | bytes 3145732
  277.3 59.5 %copy-start.3 = (f32[16,8,8,256]{3,2,1,0:T(8,128)S(1)}, f32[16,8,8,256]{3,2,1,0:T(8,128)}, u32[]{:S(2)}) copy-start(f32[16,8,8,256]{3,2,1,0:T(8,128)} %copy-done.2) | copy-start | bytes 3145732
  303.6 1.3 copy-start.4
  332.2 1.3 copy-start.5
  388.2 106.8 %copy-start.1 = (bf16[8,16,256,8]{2,3,1,0:T(8,128)(2,1)S(1)}, bf16[8,16,256,8]{2,3,1,0:T(8,128)(2,1)}, u32[]{:S(2)}) copy-start(bf16[8,16,256,8]{2,3,1,0:T(8,128)(2,1)} %param.17) | copy-start | bytes 1572868
Sparse Core Ops, SparseCore 0:
  48.2 72.7 all-gather.6
where the time goes:
time: 509 us; the launch traced here: 502 us
  matrix products  192 us (38%)
  blocking collectives  127 us (25%)
  other arithmetic  99 us (19%)
  local copies, waits for them, and re-layouts  68 us (13%)
  between operations  14.2 us (3%)
    dot_general x16, matrix products, row_scores(): jnp.einsum('tgmc,gjmc->gjt', one_hot, lookup_row, preferred_element_type=...  179 us
    all_gather x4, blocking collectives, combined_all(): gathered = jax.tree.map(lambda a: lax.all_gather(a, axis), part)  98.9 us
    add x31, other arithmetic, combine_three(): earlier[2] * factor_one[..., None] + later[2] * factor_two[..., None]  44.7 us
    all_gather x1, blocking collectives, body(): query_all = lax.all_gather(queries, 'ctx', axis=1, tiled=True)  27.7 us
    add x31, other arithmetic, combine_three(): earlier[1] * factor_one + later[1] * factor_two  25.3 us
    add x31, other arithmetic, combine_pair(): earlier[1] * jnp.exp(earlier[0] - peak)  25.3 us
    dot_general x16, local copies, waits for them, and re-layouts, row_scores(): jnp.einsum('tgmc,gjmc->gjt', one_hot, lookup_row, preferred_element_type=...  17.3 us
    eq x16, local copies, waits for them, and re-layouts, row_scores(): code_rows[..., None] == jnp.arange(CODES, dtype=jnp.int32)  14.7 us
  transfers between devices with their start and end apart: 1, of which 0 were waited for; matrix products, arithmetic and copies ran while one was open for 53% of the time, Pallas kernels for 0%

commit v1 on v0

v1 whole, which is shorter than its diff:
```python
import functools

import jax
import jax.numpy as jnp
from jax import lax
from jax.experimental import pallas as pl
from jax.experimental.pallas import tpu as pltpu
from jax.sharding import PartitionSpec as P

H = 64
KVH = 8
HD = 128
M = 16
CODES = 256
BLK = 64
SEL = 16
N = 32
R = 16
T = 256
PAIRS = 4
NEGATIVE = -1e30
SCALE = HD ** (-0.5)
F32 = jnp.float32
BF16 = jnp.bfloat16
MESH = pl.DeviceIdType.MESH


def iota(shape, dim):
    return lax.broadcasted_iota(jnp.int32, shape, dim)


def take(table, index):
    return jnp.take_along_axis(table, index, axis=1, mode="promise_in_bounds")


def kernel(
    q_hbm, k_hbm, v_hbm, c_hbm, cb_hbm, len_hbm, blk_hbm,
    att_ref, mass_ref,
    qbuf, qf0, qf1, qp0, qp1, codes, keys, vals, cb, raw_lo, raw_hi, tab_lo, tab_hi,
    khat, lens, blk, chosen, idx_a, idx_b, guesses, scores, weights, stage, sendbuf, recvbuf, stat, stat_out, stat_in,
    q_own, small_sem, code_sem, key_sem, val_sem,
    q_send, q_recv, o_send, o_recv, s_send, s_recv,
):
    me = lax.axis_index("ctx")

    own_q = pltpu.make_async_copy(q_hbm, q_own, small_sem.at[0])
    book = pltpu.make_async_copy(cb_hbm, cb, small_sem.at[1])
    lengths = pltpu.make_async_copy(len_hbm, lens, small_sem.at[2])
    selected = pltpu.make_async_copy(blk_hbm, blk, small_sem.at[3])
    for copy in (own_q, book, lengths, selected):
        copy.start()

    def copy_of(source, target, sem, r):
        return pltpu.make_async_copy(source.at[r], target.at[r], sem.at[r])

    def start_rows(source, target, sem):
        def step(r, carry):
            copy_of(source, target, sem, r).start()
            return carry

        lax.fori_loop(0, R, step, 0)

    start_rows(c_hbm, codes, code_sem)

    barrier = pltpu.get_barrier_semaphore()

    def greet(k, carry):
        pl.semaphore_signal(
            barrier, inc=1, device_id={"ctx": lax.rem(me + k, N)}, device_id_type=MESH
        )
        return carry

    lax.fori_loop(1, N, greet, 0)
    start_rows(k_hbm, keys, key_sem)
    start_rows(v_hbm, vals, val_sem)
    own_q.wait()
    qbuf[me] = q_own[...]
    pl.semaphore_wait(barrier, N - 1)

    def send_query(k, carry):
        pltpu.make_async_remote_copy(
            src_ref=q_own,
            dst_ref=qbuf.at[me],
            send_sem=q_send,
            recv_sem=q_recv,
            device_id={"ctx": lax.rem(me + k, N)},
            device_id_type=MESH,
        ).start()
        return carry

    lax.fori_loop(1, N, send_query, 0)

    book.wait()

    def widen(i, carry):
        rows = pl.ds(pl.multiple_of(i * 64, 64), 64)
        wide = cb[rows, :].astype(F32)
        raw_lo[rows, :] = wide[:, :128]
        raw_hi[rows, :] = wide[:, 128:]
        for s in range(8):
            spread = pl.ds(i * 64 + s, 8, stride=8)
            packed = pl.ds(pl.multiple_of(i * 64 + s * 8, 8), 8)
            tab_lo[packed, :] = raw_lo[spread, :]
            tab_hi[packed, :] = raw_hi[spread, :]
        return carry

    lax.fori_loop(0, 16, widen, 0)

    lengths.wait()
    selected.wait()
    names = blk[...].reshape(R * KVH, SEL)
    total = jnp.zeros((R * KVH, T), F32)
    for b in range(T // BLK):
        hit = (names == me * (T // BLK) + b).astype(F32).astype(BF16)
        spot = (iota((SEL, T), 1) // BLK == b).astype(F32).astype(BF16)
        total = total + jnp.dot(hit, spot, preferred_element_type=F32)
    chosen[...] = total

    def decode_row(r, index):
        for i in range(16):
            columns = []
            code = index[i * 8 : i * 8 + 8, :]
            for half in range(2):
                part = code[:, half * 128 : half * 128 + 128]
                low = part & 127
                high = part > 127
                parts = []
                for s in range(8):
                    at = (i * 8 + s) * 8
                    parts.append(
                        jnp.where(
                            high, take(tab_hi[at : at + 8, :], low), take(tab_lo[at : at + 8, :], low)
                        )
                    )
                columns.append(jnp.concatenate(parts, axis=0))
            khat[r, i * 64 : i * 64 + 64, :] = jnp.concatenate(columns, axis=1).astype(BF16)

    copy_of(c_hbm, codes, code_sem, 0).wait()
    idx_a[...] = codes[0].T

    def decode_two(n, carry):
        copy_of(c_hbm, codes, code_sem, 2 * n + 1).wait()

        @pl.when(n < R // 2 - 1)
        def _():
            copy_of(c_hbm, codes, code_sem, 2 * n + 2).wait()

        idx_b[...] = codes[2 * n + 1].T
        decode_row(2 * n, idx_a)
        idx_a[...] = codes[jnp.minimum(2 * n + 2, R - 1)].T
        decode_row(2 * n + 1, idx_b)
        return carry

    lax.fori_loop(0, R // 2, decode_two, 0)

    whole = qbuf.at[pl.ds(0, N - 1)]
    pltpu.make_async_copy(whole, whole, q_recv).wait()
    pltpu.make_async_copy(whole, whole, q_send).wait()
    to_row = iota((HD, HD), 0)
    to_col = iota((HD, HD), 1)
    origin = (to_col & 64) | ((to_col & 7) << 3) | ((to_col >> 3) & 7)
    permute = (to_row == origin).astype(F32).astype(BF16)
    for hh, (plain, turned) in enumerate(((qf0, qp0), (qf1, qp1))):
        part = qbuf[:, :, hh * HD : hh * HD + HD].reshape(N * R, HD)
        plain[...] = part.astype(F32)
        turned[...] = jnp.dot(part, permute, preferred_element_type=F32)

    def wait_rows(r, carry):
        copy_of(k_hbm, keys, key_sem, r).wait()
        copy_of(v_hbm, vals, val_sem, r).wait()
        return carry

    lax.fori_loop(0, R, wait_rows, 0)

    left = (iota((16, 1), 0) & 7) < 4
    left_wide = (iota((16, HD), 0) & 7) < 4
    position = iota((1, T), 1) + me * T
    lane = iota((8, 128), 1)

    def spread_heads(part0, part1, r, p):
        at = pl.ds(p * 128 + r, 8, stride=16)
        both = jnp.concatenate([part0[at, :], part1[at, :]], axis=0)
        return jnp.concatenate(
            [jnp.where(left_wide, both, 0.0), jnp.where(left_wide, 0.0, both)], axis=1
        ).astype(BF16)

    def place(n):
        step = n // 4
        turn = jnp.where(lax.rem(me, 2) == 0, step + 1, 3 - step)
        return lax.rem(me // 8 + turn, PAIRS), lax.rem(n, 4) * 4

    def multiply(n):
        p, first = place(n)
        wide = pl.ds(pl.multiple_of(p * 256, 256), 256)
        for u in range(4):
            r = first + u
            at = slice(u * 16, u * 16 + 16)
            guesses[at, :] = jnp.dot(
                spread_heads(qp0, qp1, r, p), khat[r, wide, :], preferred_element_type=F32
            )
            scores[at, :] = lax.dot_general(
                spread_heads(qf0, qf1, r, p),
                keys[r, :, wide],
                (((1,), (1,)), ((), ())),
                preferred_element_type=F32,
            )

    def weigh(n):
        p, first = place(n)
        eight = pl.ds(pl.multiple_of(p * 8, 8), 8)
        kept = stat[eight, :]
        for u in range(4):
            r = first + u
            at = slice(u * 16, u * 16 + 16)
            inside = position < lens[r]
            guess = jnp.where(inside, guesses[at, :] * SCALE, NEGATIVE)
            guess_peak = jnp.max(guess, axis=1, keepdims=True)
            guess_total = jnp.sum(
                jnp.where(inside, jnp.exp(guess - guess_peak), 0.0), axis=1, keepdims=True
            )
            here = chosen[pl.ds(r * KVH + 2 * p, 1), :]
            there = chosen[pl.ds(r * KVH + 2 * p + 1, 1), :]
            used = (jnp.where(left, here, there) > 0.5) & inside
            score = jnp.where(used, scores[at, :] * SCALE, NEGATIVE)
            peak = jnp.max(score, axis=1, keepdims=True)
            weight = jnp.where(used, jnp.exp(score - peak), 0.0)
            weight_total = jnp.sum(weight, axis=1, keepdims=True)
            weights[at, :] = weight.astype(BF16)
            for kind, value in enumerate((guess_peak, guess_total, peak, weight_total)):
                for hh in range(2):
                    kept = jnp.where(
                        lane == kind * 32 + hh * 16 + r, value[hh * 8 : hh * 8 + 8], kept
                    )
        stat[eight, :] = kept

    def average(n):
        p, first = place(n)
        wide = pl.ds(pl.multiple_of(p * 256, 256), 256)
        for u in range(4):
            r = first + u
            summed = jnp.dot(
                weights[u * 16 : u * 16 + 16, :], vals[r, :, wide], preferred_element_type=F32
            )
            summed = jnp.where(left, summed[:, :HD], summed[:, HD:])
            stage[pl.ds(p * 256 + r, 8, stride=32), :] = summed[:8]
            stage[pl.ds(p * 256 + 16 + r, 8, stride=32), :] = summed[8:]

    def send_parts(n):
        p, _ = place(n)
        block = pl.ds(pl.multiple_of(p * 256, 256), 256)
        sendbuf[block, :] = stage[block, :].astype(BF16)
        for k in range(8):
            stat_out[p * 8 + k] = stat[pl.ds(p * 8 + k, 1), :]

        def send_to(k, inner):
            to = p * 8 + k

            @pl.when(to != me)
            def _():
                pltpu.make_async_remote_copy(
                    src_ref=stat_out.at[to],
                    dst_ref=stat_in.at[me],
                    send_sem=s_send,
                    recv_sem=s_recv,
                    device_id={"ctx": to},
                    device_id_type=MESH,
                ).start()
                pltpu.make_async_remote_copy(
                    src_ref=sendbuf.at[pl.ds(pl.multiple_of(to * 32, 32), 32)],
                    dst_ref=recvbuf.at[pl.ds(pl.multiple_of(me * 32, 32), 32)],
                    send_sem=o_send,
                    recv_sem=o_recv,
                    device_id={"ctx": to},
                    device_id_type=MESH,
                ).start()

            return inner

        lax.fori_loop(0, 8, send_to, 0)

    multiply(0)
    weigh(0)
    multiply(1)

    def attend(n, carry):
        average(n - 2)
        weigh(n - 1)
        multiply(n)

        @pl.when(lax.rem(n, 4) == 1)
        def _():
            send_parts(n - 2)

        return carry

    lax.fori_loop(2, R, attend, 0)
    average(R - 2)
    weigh(R - 1)
    average(R - 1)
    send_parts(R - 1)
    mine = pl.ds(pl.multiple_of(me * 32, 32), 32)
    recvbuf[mine, :] = sendbuf[mine, :]
    stat_in[me] = stat_out[me]

    some = stat_in.at[pl.ds(0, N - 1)]
    pltpu.make_async_copy(some, some, s_recv).wait()
    stats = stat_in[...].reshape(N, 128)
    top = jnp.max(stats, axis=0, keepdims=True)
    factor = jnp.exp(stats - top)
    totals = jnp.sum(factor * pltpu.roll(stats, 96, 1), axis=0, keepdims=True)
    mass = top + jnp.log(totals)
    mass_ref[0:1, :] = mass[:, 0:16]
    mass_ref[1:2, :] = mass[:, 16:32]
    share = (factor / totals)[:, 64:96].T
    source = iota((N, N * 32), 1) // 32
    spread = (source == iota((N, N * 32), 0)).astype(F32).astype(BF16)
    mix = jnp.dot(share.astype(BF16), spread, preferred_element_type=F32)
    same = (iota((32, N * 32), 1) & 31) == iota((32, N * 32), 0)
    mix = jnp.where(same, mix, 0.0).astype(BF16)
    some = recvbuf.at[pl.ds(0, (N - 1) * 32)]
    pltpu.make_async_copy(some, some, o_recv).wait()
    result = jnp.dot(mix, recvbuf[...], preferred_element_type=F32)
    att_ref[:, 0:HD] = result[:R].astype(BF16)
    att_ref[:, HD:] = result[R:].astype(BF16)
    some = stat_in.at[pl.ds(0, N - 1)]
    pltpu.make_async_copy(some, some, s_send).wait()
    some = recvbuf.at[pl.ds(0, (N - 1) * 32)]
    pltpu.make_async_copy(some, some, o_send).wait()


def body(queries, keys, values, codes, codebook, lengths, blocks):
    book = codebook.transpose(0, 1, 3, 2).reshape(KVH * M * 8, CODES)
    anywhere = pl.BlockSpec(memory_space=pl.ANY)
    vmem = pl.BlockSpec(memory_space=pltpu.VMEM)
    dma = pltpu.SemaphoreType.DMA
    attended, mass = pl.pallas_call(
        kernel,
        out_shape=(
            jax.ShapeDtypeStruct((R, 2 * HD), BF16),
            jax.ShapeDtypeStruct((2, R), F32),
        ),
        in_specs=[anywhere] * 7,
        out_specs=(vmem, vmem),
        scratch_shapes=[
            pltpu.VMEM((N, R, 2 * HD), BF16),
            pltpu.VMEM((N * R, HD), F32),
            pltpu.VMEM((N * R, HD), F32),
            pltpu.VMEM((N * R, HD), F32),
            pltpu.VMEM((N * R, HD), F32),
            pltpu.VMEM((R, T, KVH * M), jnp.int32),
            pltpu.VMEM((R, T, KVH * HD), BF16),
            pltpu.VMEM((R, T, KVH * HD), BF16),
            pltpu.VMEM((KVH * M * 8, CODES), BF16),
            pltpu.VMEM((KVH * M * 8, 128), F32),
            pltpu.VMEM((KVH * M * 8, 128), F32),
            pltpu.VMEM((KVH * M * 8, 128), F32),
            pltpu.VMEM((KVH * M * 8, 128), F32),
            pltpu.VMEM((R, KVH * HD, T), BF16),
            pltpu.SMEM((R,), jnp.int32),
            pltpu.VMEM((R, KVH, SEL), jnp.int32),
            pltpu.VMEM((R * KVH, T), F32),
            pltpu.VMEM((KVH * M, T), jnp.int32),
            pltpu.VMEM((KVH * M, T), jnp.int32),
            pltpu.VMEM((64, T), F32),
            pltpu.VMEM((64, T), F32),
            pltpu.VMEM((64, T), BF16),
            pltpu.VMEM((N * 32, HD), F32),
            pltpu.VMEM((N * 32, HD), BF16),
            pltpu.VMEM((N * 32, HD), BF16),
            pltpu.VMEM((N, 128), F32),
            pltpu.VMEM((N, 1, 128), F32),
            pltpu.VMEM((N, 1, 128), F32),
            pltpu.VMEM((R, 2 * HD), BF16),
            dma((4,)),
            dma((R,)),
            dma((R,)),
            dma((R,)),
            dma, dma, dma, dma, dma, dma,
        ],
        compiler_params=pltpu.CompilerParams(
            collective_id=0, has_side_effects=True, vmem_limit_bytes=62 * 2**20
        ),
        name="decode_attention",
    )(queries, keys, values, codes, book, lengths, blocks)
    return attended, mass.T


def solution(mesh):
    placed = (
        P("rows", "ctx"),
        P("rows", "ctx", None),
        P("rows", "ctx", None),
        P("rows", "ctx", None),
        P(),
        P("rows"),
        P("rows", None, None),
    )
    return jax.shard_map(
        body,
        mesh=mesh,
        in_specs=placed,
        out_specs=(P("rows", "ctx"), P("rows", "ctx")),
        check_vma=False,
    )
```

time: 509 us -> 30.5 us (0.06); the launches traced: 502 us -> 30.3 us
  matrix products: 192 us -> 0 us
  blocking collectives: 127 us -> 0 us
  other arithmetic: 99 us -> 0 us
  local copies, waits for them, and re-layouts: 68 us -> 2.51 us
  Pallas kernels: 0 us -> 27.2 us
  between operations: 14.2 us -> 0.64 us
    dot_general x19 -> x0, matrix products: 192 us -> none  [the longest x16 179 us: row_scores(): jnp.einsum('tgmc,gjmc->gjt', one_hot, lookup_row, preferred_element_type=...]
    all_gather x5 -> x0, blocking collectives: 127 us -> none  [the longest x4 98.9 us: combined_all(): gathered = jax.tree.map(lambda a: lax.all_gather(a, axis), part)]
    add x93 -> x0, other arithmetic: 95.2 us -> none  [the longest x31 44.7 us: combine_three(): earlier[2] * factor_one[..., None] + later[2] * factor_two[..., None]]
    pallas_call x0 -> x1, Pallas kernels: none -> 27.2 us  [body(): pl.pallas_call(kernel, out_shape=(jax.ShapeDtypeStruct((R, 2 * HD), BF16)...]
    while x10 -> x0, local copies, waits for them, and re-layouts: 19.7 us -> none  [the longest x9 10 us: combined_all(): lax.fori_loop(1, lax.axis_size(axis), lambda source, state: combine(state...]
    dot_general x16 -> x0, local copies, waits for them, and re-layouts: 17.3 us -> none  [row_scores(): jnp.einsum('tgmc,gjmc->gjt', one_hot, lookup_row, preferred_element_type=...]
    eq x16 -> x0, local copies, waits for them, and re-layouts: 14.7 us -> none  [row_scores(): code_rows[..., None] == jnp.arange(CODES, dtype=jnp.int32)]
    exp x62 -> x0, local copies, waits for them, and re-layouts: 5.32 us -> none  [the longest x31 2.68 us: combine_three(): factor_one = jnp.exp(earlier[0] - peak)]
  transfers between devices with their start and end apart: 1 -> 0, of which waited for: 0 -> 0; matrix products, arithmetic and copies ran while one was open for 53% -> 0% of each run, Pallas kernels for 0% -> 0%
where the time goes in v1:
time: 30.5 us; the launch traced here: 30.3 us
  Pallas kernels  27.2 us (89%)
  local copies, waits for them, and re-layouts  2.51 us (8%)
  between operations  0.64 us (2%)
    pallas_call x1, Pallas kernels, body(): pl.pallas_call(kernel, out_shape=(jax.ShapeDtypeStruct((R, 2 * HD), BF16)...  27.2 us
    unnamed x2, local copies, waits for them, and re-layouts  2.51 us

profile of v1, /device:TPU:1, one launch (start us, length us, event | category | flops | bytes accessed | tf_op | source)
XLA Modules:
  0.0 30.3 jit_solution(17548765599047214331)
XLA Ops:
  0.6 27.2 %decode_attention.1 = (bf16[16,256]{1,0:T(8,128)(2,1)}, f32[2,16]{1,0:T(2,128)}) custom-call(bf16[16,256]{1,0:T(8,128)(2,1)} %q_hbm.1, bf16[16,256,1024]{2,1,0:T(8,128)(2,1)} %k_hbm.1, bf16[16,256,1024]{2,1,0:T(8,128)(2,1)} %v_hbm.1, s32[16,256,128]{2,1,0:T(8,128)} %c_hbm.1, bf16[1024,256]{1,0:T(8,128)(2,1)} %bitcast.4, s32[16]{0:T(128)} %len_hbm.1, ...), custom_call_target="tpu_custom_call" | custom-call | tf_op jit(solution)/shard_map/decode_attention/pallas_call | solution.py:336
  27.8 1.3 %copy.11 = bf16[16,256]{1,0:T(8,128)(2,1)} copy(bf16[16,256]{1,0:T(8,128)(2,1)} %get-tuple-element.8) | data formatting | bytes 16384
  29.1 1.2 %copy.12 = f32[16,2]{0,1:T(2,128)} copy(f32[16,2]{0,1:T(2,128)} %bitcast.5) | data formatting | bytes 256

commit v2 on v1

--- a/solution.py
+++ b/solution.py
@@ -18,6 +18,7 @@
 R = 16
 T = 256
 PAIRS = 4
+EARLY = 2
 NEGATIVE = -1e30
 SCALE = HD ** (-0.5)
 F32 = jnp.float32
@@ -43,25 +44,6 @@
 ):
     me = lax.axis_index("ctx")
 
-    own_q = pltpu.make_async_copy(q_hbm, q_own, small_sem.at[0])
-    book = pltpu.make_async_copy(cb_hbm, cb, small_sem.at[1])
-    lengths = pltpu.make_async_copy(len_hbm, lens, small_sem.at[2])
-    selected = pltpu.make_async_copy(blk_hbm, blk, small_sem.at[3])
-    for copy in (own_q, book, lengths, selected):
-        copy.start()
-
-    def copy_of(source, target, sem, r):
-        return pltpu.make_async_copy(source.at[r], target.at[r], sem.at[r])
-
-    def start_rows(source, target, sem):
-        def step(r, carry):
-            copy_of(source, target, sem, r).start()
-            return carry
-
-        lax.fori_loop(0, R, step, 0)
-
-    start_rows(c_hbm, codes, code_sem)
-
     barrier = pltpu.get_barrier_semaphore()
 
     def greet(k, carry):
@@ -71,24 +53,28 @@
         return carry
 
     lax.fori_loop(1, N, greet, 0)
-    start_rows(k_hbm, keys, key_sem)
-    start_rows(v_hbm, vals, val_sem)
+
+    own_q = pltpu.make_async_copy(q_hbm, q_own, small_sem.at[0])
+    book = pltpu.make_async_copy(cb_hbm, cb, small_sem.at[1])
+    lengths = pltpu.make_async_copy(len_hbm, lens, small_sem.at[2])
+    selected = pltpu.make_async_copy(blk_hbm, blk, small_sem.at[3])
+
+    def two_codes(n):
+        rows = pl.ds(2 * n, 2)
+        return pltpu.make_async_copy(c_hbm.at[rows], codes.at[rows], code_sem.at[n])
+
+    all_keys = pltpu.make_async_copy(k_hbm, keys, key_sem)
+    all_vals = pltpu.make_async_copy(v_hbm, vals, val_sem)
+    book.start()
+    two_codes(0).start()
+    for copy in (own_q, lengths, selected):
+        copy.start()
+    for n in range(1, R // 2):
+        two_codes(n).start()
+    all_keys.start()
+    all_vals.start()
     own_q.wait()
     qbuf[me] = q_own[...]
-    pl.semaphore_wait(barrier, N - 1)
-
-    def send_query(k, carry):
-        pltpu.make_async_remote_copy(
-            src_ref=q_own,
-            dst_ref=qbuf.at[me],
-            send_sem=q_send,
-            recv_sem=q_recv,
-            device_id={"ctx": lax.rem(me + k, N)},
-            device_id_type=MESH,
-        ).start()
-        return carry
-
-    lax.fori_loop(1, N, send_query, 0)
 
     book.wait()
 
@@ -135,15 +121,13 @@
                 columns.append(jnp.concatenate(parts, axis=0))
             khat[r, i * 64 : i * 64 + 64, :] = jnp.concatenate(columns, axis=1).astype(BF16)
 
-    copy_of(c_hbm, codes, code_sem, 0).wait()
+    two_codes(0).wait()
     idx_a[...] = codes[0].T
 
     def decode_two(n, carry):
-        copy_of(c_hbm, codes, code_sem, 2 * n + 1).wait()
-
         @pl.when(n < R // 2 - 1)
         def _():
-            copy_of(c_hbm, codes, code_sem, 2 * n + 2).wait()
+            two_codes(n + 1).wait()
 
         idx_b[...] = codes[2 * n + 1].T
         decode_row(2 * n, idx_a)
@@ -151,7 +135,23 @@
         decode_row(2 * n + 1, idx_b)
         return carry
 
-    lax.fori_loop(0, R // 2, decode_two, 0)
+    lax.fori_loop(0, EARLY, decode_two, 0)
+    pl.semaphore_wait(barrier, N - 1)
+
+    def send_query(k, carry):
+        pltpu.make_async_remote_copy(
+            src_ref=q_own,
+            dst_ref=qbuf.at[me],
+            send_sem=q_send,
+            recv_sem=q_recv,
+            device_id={"ctx": lax.rem(me + k, N)},
+            device_id_type=MESH,
+        ).start()
+        return carry
+
+    lax.fori_loop(1, N, send_query, 0)
+
+    lax.fori_loop(EARLY, R // 2, decode_two, 0)
 
     whole = qbuf.at[pl.ds(0, N - 1)]
     pltpu.make_async_copy(whole, whole, q_recv).wait()
@@ -165,13 +165,8 @@
         plain[...] = part.astype(F32)
         turned[...] = jnp.dot(part, permute, preferred_element_type=F32)
 
-    def wait_rows(r, carry):
-        copy_of(k_hbm, keys, key_sem, r).wait()
-        copy_of(v_hbm, vals, val_sem, r).wait()
-        return carry
-
-    lax.fori_loop(0, R, wait_rows, 0)
-
+    all_keys.wait()
+    all_vals.wait()
     left = (iota((16, 1), 0) & 7) < 4
     left_wide = (iota((16, HD), 0) & 7) < 4
     position = iota((1, T), 1) + me * T
@@ -372,9 +367,8 @@
             pltpu.VMEM((N, 1, 128), F32),
             pltpu.VMEM((R, 2 * HD), BF16),
             dma((4,)),
-            dma((R,)),
-            dma((R,)),
-            dma((R,)),
+            dma((R // 2,)),
+            dma, dma,
             dma, dma, dma, dma, dma, dma,
         ],
         compiler_params=pltpu.CompilerParams(
@@ -382,6 +376,26 @@
         ),
         name="decode_attention",
     )(queries, keys, values, codes, book, lengths, blocks)
+
+    def hand_over(from_attended, from_mass, to_attended, to_mass, sems):
+        first = pltpu.make_async_copy(from_attended, to_attended, sems.at[0])
+        second = pltpu.make_async_copy(from_mass, to_mass, sems.at[1])
+        first.start()
+        second.start()
+        first.wait()
+        second.wait()
+
+    attended, mass = pl.pallas_call(
+        hand_over,
+        out_shape=(
+            jax.ShapeDtypeStruct((R, 2 * HD), BF16),
+            jax.ShapeDtypeStruct((2, R), F32),
+        ),
+        in_specs=[anywhere] * 2,
+        out_specs=(anywhere, anywhere),
+        scratch_shapes=[dma((2,))],
+        name="hand_over",
+    )(attended, mass)
     return attended, mass.T
 
 

time: 30.5 us -> 27.7 us (0.908)
  local copies, waits for them, and re-layouts: 2.51 us -> 0 us
    unnamed x2 -> x0, local copies, waits for them, and re-layouts: 2.51 us -> none
    pallas_call x1, Pallas kernels: 27.2 us -> 25.6 us  [body(): pl.pallas_call(kernel, out_shape=(jax.ShapeDtypeStruct((R, 2 * HD), BF16)...]
    pallas_call x0 -> x1, Pallas kernels: none -> 1.4 us  [body(): pl.pallas_call(hand_over, out_shape=(jax.ShapeDtypeStruct((R, 2 * HD), BF...]
where the time goes in v2:
time: 27.7 us; the launch traced here: 27.6 us
  Pallas kernels  27 us (97%)
  between operations  0.64 us (2%)
    pallas_call x1, Pallas kernels, body(): pl.pallas_call(kernel, out_shape=(jax.ShapeDtypeStruct((R, 2 * HD), BF16)...  25.6 us
    pallas_call x1, Pallas kernels, body(): pl.pallas_call(hand_over, out_shape=(jax.ShapeDtypeStruct((R, 2 * HD), BF...  1.4 us

profile of v2, /device:TPU:1, one launch (start us, length us, event | category | flops | bytes accessed | tf_op | source)
XLA Modules:
  0.0 27.6 jit_solution(14035965424754932830)
XLA Ops:
  0.6 25.6 %decode_attention.1 = (bf16[16,256]{1,0:T(8,128)(2,1)}, f32[2,16]{1,0:T(2,128)}) custom-call(bf16[16,256]{1,0:T(8,128)(2,1)} %q_hbm.1, bf16[16,256,1024]{2,1,0:T(8,128)(2,1)} %k_hbm.1, bf16[16,256,1024]{2,1,0:T(8,128)(2,1)} %v_hbm.1, s32[16,256,128]{2,1,0:T(8,128)} %c_hbm.1, bf16[1024,256]{1,0:T(8,128)(2,1)} %bitcast.4, s32[16]{0:T(128)} %len_hbm.1, ...), custom_call_target="tpu_custom_call" | custom-call | tf_op jit(solution)/shard_map/decode_attention/pallas_call | solution.py:331
  26.2 1.4 %hand_over.1 = (bf16[16,256]{1,0:T(8,128)(2,1)}, f32[2,16]{1,0:T(2,128)}) custom-call(bf16[16,256]{1,0:T(8,128)(2,1)} %get-tuple-element.6.from_attended, f32[2,16]{1,0:T(2,128)} %get-tuple-element.7.from_mass), custom_call_target="tpu_custom_call" | custom-call | tf_op jit(solution)/shard_map/hand_over/pallas_call | solution.py:388

commit v3 on v2

--- a/solution.py
+++ b/solution.py
@@ -18,7 +18,7 @@
 R = 16
 T = 256
 PAIRS = 4
-EARLY = 2
+EARLY = 1
 NEGATIVE = -1e30
 SCALE = HD ** (-0.5)
 F32 = jnp.float32
@@ -38,7 +38,7 @@
     q_hbm, k_hbm, v_hbm, c_hbm, cb_hbm, len_hbm, blk_hbm,
     att_ref, mass_ref,
     qbuf, qf0, qf1, qp0, qp1, codes, keys, vals, cb, raw_lo, raw_hi, tab_lo, tab_hi,
-    khat, lens, blk, chosen, idx_a, idx_b, guesses, scores, weights, stage, sendbuf, recvbuf, stat, stat_out, stat_in,
+    khat, lens, blk, chosen, idx_a, idx_b, idx_c, idx_d, guesses, scores, weights, stage, sendbuf, recvbuf, stat, stat_out, stat_in,
     q_own, small_sem, code_sem, key_sem, val_sem,
     q_send, q_recv, o_send, o_recv, s_send, s_recv,
 ):
@@ -122,20 +122,27 @@
             khat[r, i * 64 : i * 64 + 64, :] = jnp.concatenate(columns, axis=1).astype(BF16)
 
     two_codes(0).wait()
+    two_codes(1).wait()
     idx_a[...] = codes[0].T
 
-    def decode_two(n, carry):
-        @pl.when(n < R // 2 - 1)
+    def decode_four(n, carry):
+        @pl.when(n < R // 4 - 1)
         def _():
-            two_codes(n + 1).wait()
-
-        idx_b[...] = codes[2 * n + 1].T
-        decode_row(2 * n, idx_a)
-        idx_a[...] = codes[jnp.minimum(2 * n + 2, R - 1)].T
-        decode_row(2 * n + 1, idx_b)
+            two_codes(2 * n + 2).wait()
+            two_codes(2 * n + 3).wait()
+
+        r = 4 * n
+        idx_b[...] = codes[r + 1].T
+        decode_row(r, idx_a)
+        idx_c[...] = codes[r + 2].T
+        decode_row(r + 1, idx_b)
+        idx_d[...] = codes[r + 3].T
+        decode_row(r + 2, idx_c)
+        idx_a[...] = codes[jnp.minimum(r + 4, R - 1)].T
+        decode_row(r + 3, idx_d)
         return carry
 
-    lax.fori_loop(0, EARLY, decode_two, 0)
+    lax.fori_loop(0, EARLY, decode_four, 0)
     pl.semaphore_wait(barrier, N - 1)
 
     def send_query(k, carry):
@@ -151,7 +158,7 @@
 
     lax.fori_loop(1, N, send_query, 0)
 
-    lax.fori_loop(EARLY, R // 2, decode_two, 0)
+    lax.fori_loop(EARLY, R // 4, decode_four, 0)
 
     whole = qbuf.at[pl.ds(0, N - 1)]
     pltpu.make_async_copy(whole, whole, q_recv).wait()
@@ -240,10 +247,8 @@
             stage[pl.ds(p * 256 + r, 8, stride=32), :] = summed[:8]
             stage[pl.ds(p * 256 + 16 + r, 8, stride=32), :] = summed[8:]
 
-    def send_parts(n):
+    def send_stats(n):
         p, _ = place(n)
-        block = pl.ds(pl.multiple_of(p * 256, 256), 256)
-        sendbuf[block, :] = stage[block, :].astype(BF16)
         for k in range(8):
             stat_out[p * 8 + k] = stat[pl.ds(p * 8 + k, 1), :]
 
@@ -260,6 +265,21 @@
                     device_id={"ctx": to},
                     device_id_type=MESH,
                 ).start()
+
+            return inner
+
+        lax.fori_loop(0, 8, send_to, 0)
+
+    def send_values(n):
+        p, _ = place(n)
+        block = pl.ds(pl.multiple_of(p * 256, 256), 256)
+        sendbuf[block, :] = stage[block, :].astype(BF16)
+
+        def send_to(k, inner):
+            to = p * 8 + k
+
+            @pl.when(to != me)
+            def _():
                 pltpu.make_async_remote_copy(
                     src_ref=sendbuf.at[pl.ds(pl.multiple_of(to * 32, 32), 32)],
                     dst_ref=recvbuf.at[pl.ds(pl.multiple_of(me * 32, 32), 32)],
@@ -284,19 +304,23 @@
 
         @pl.when(lax.rem(n, 4) == 1)
         def _():
-            send_parts(n - 2)
+            send_stats(n - 2)
+            send_values(n - 2)
 
         return carry
 
     lax.fori_loop(2, R, attend, 0)
     average(R - 2)
     weigh(R - 1)
+    send_stats(R - 1)
     average(R - 1)
-    send_parts(R - 1)
+    send_values(R - 1)
     mine = pl.ds(pl.multiple_of(me * 32, 32), 32)
     recvbuf[mine, :] = sendbuf[mine, :]
     stat_in[me] = stat_out[me]
 
+    source = iota((N, N * 32), 1) // 32
+    spread = (source == iota((N, N * 32), 0)).astype(F32).astype(BF16)
     some = stat_in.at[pl.ds(0, N - 1)]
     pltpu.make_async_copy(some, some, s_recv).wait()
     stats = stat_in[...].reshape(N, 128)
@@ -307,8 +331,6 @@
     mass_ref[0:1, :] = mass[:, 0:16]
     mass_ref[1:2, :] = mass[:, 16:32]
     share = (factor / totals)[:, 64:96].T
-    source = iota((N, N * 32), 1) // 32
-    spread = (source == iota((N, N * 32), 0)).astype(F32).astype(BF16)
     mix = jnp.dot(share.astype(BF16), spread, preferred_element_type=F32)
     same = (iota((32, N * 32), 1) & 31) == iota((32, N * 32), 0)
     mix = jnp.where(same, mix, 0.0).astype(BF16)
@@ -331,8 +353,8 @@
     attended, mass = pl.pallas_call(
         kernel,
         out_shape=(
-            jax.ShapeDtypeStruct((R, 2 * HD), BF16),
-            jax.ShapeDtypeStruct((2, R), F32),
+            pltpu.VMEM((R, 2 * HD), BF16),
+            pltpu.VMEM((2, R), F32),
         ),
         in_specs=[anywhere] * 7,
         out_specs=(vmem, vmem),
@@ -356,6 +378,8 @@
             pltpu.VMEM((R * KVH, T), F32),
             pltpu.VMEM((KVH * M, T), jnp.int32),
             pltpu.VMEM((KVH * M, T), jnp.int32),
+            pltpu.VMEM((KVH * M, T), jnp.int32),
+            pltpu.VMEM((KVH * M, T), jnp.int32),
             pltpu.VMEM((64, T), F32),
             pltpu.VMEM((64, T), F32),
             pltpu.VMEM((64, T), BF16),
@@ -372,30 +396,11 @@
             dma, dma, dma, dma, dma, dma,
         ],
         compiler_params=pltpu.CompilerParams(
-            collective_id=0, has_side_effects=True, vmem_limit_bytes=62 * 2**20
+            collective_id=0, has_side_effects=True, vmem_limit_bytes=56 * 2**20
         ),
         name="decode_attention",
     )(queries, keys, values, codes, book, lengths, blocks)
 
-    def hand_over(from_attended, from_mass, to_attended, to_mass, sems):
-        first = pltpu.make_async_copy(from_attended, to_attended, sems.at[0])
-        second = pltpu.make_async_copy(from_mass, to_mass, sems.at[1])
-        first.start()
-        second.start()
-        first.wait()
-        second.wait()
-
-    attended, mass = pl.pallas_call(
-        hand_over,
-        out_shape=(
-            jax.ShapeDtypeStruct((R, 2 * HD), BF16),
-            jax.ShapeDtypeStruct((2, R), F32),
-        ),
-        in_specs=[anywhere] * 2,
-        out_specs=(anywhere, anywhere),
-        scratch_shapes=[dma((2,))],
-        name="hand_over",
-    )(attended, mass)
     return attended, mass.T
 
 

time: 27.7 us -> 26.7 us (0.964)
  Pallas kernels: 27 us -> 24.8 us
  local copies, waits for them, and re-layouts: 0 us -> 1.16 us
    pallas_call x2 -> x1, Pallas kernels: 27 us -> 24.8 us  [body(): pl.pallas_call(kernel, out_shape=(pltpu.VMEM((R, 2 * HD), BF16), pltpu.VM...]
    unnamed x0 -> x2, local copies, waits for them, and re-layouts: none -> 1.16 us
where the time goes in v3:
time: 26.7 us; the launch traced here: 26.6 us
  Pallas kernels  24.8 us (93%)
  local copies, waits for them, and re-layouts  1.16 us (4%)
  between operations  0.64 us (2%)
    pallas_call x1, Pallas kernels, body(): pl.pallas_call(kernel, out_shape=(pltpu.VMEM((R, 2 * HD), BF16), pltpu.VM...  24.8 us
    unnamed x2, local copies, waits for them, and re-layouts  1.16 us

profile of v3, /device:TPU:1, one launch (start us, length us, event | category | flops | bytes accessed | tf_op | source)
XLA Modules:
  0.0 26.6 jit_solution(14427897082977510325)
XLA Ops:
  0.6 24.8 %decode_attention.1 = (bf16[16,256]{1,0:T(8,128)(2,1)S(1)}, f32[2,16]{1,0:T(2,128)S(1)}) custom-call(bf16[16,256]{1,0:T(8,128)(2,1)} %q_hbm.1, bf16[16,256,1024]{2,1,0:T(8,128)(2,1)} %k_hbm.1, bf16[16,256,1024]{2,1,0:T(8,128)(2,1)} %v_hbm.1, s32[16,256,128]{2,1,0:T(8,128)} %c_hbm.1, bf16[1024,256]{1,0:T(8,128)(2,1)} %bitcast.5, s32[16]{0:T(128)} %len_hbm.1, ...), custom_call_target="tpu_custom_call" | custom-call | tf_op jit(solution)/shard_map/decode_attention/pallas_call | solution.py:353
  25.4 0.6 %copy.11 = bf16[16,256]{1,0:T(8,128)(2,1)} copy(bf16[16,256]{1,0:T(8,128)(2,1)S(1)} %get-tuple-element.6) | data formatting | bytes 16384
  26.0 0.6 %copy.12 = f32[16,2]{0,1:T(2,128)} copy(f32[16,2]{0,1:T(2,128)S(1)} %bitcast.4) | data formatting | bytes 256

commit v4 on v3

--- a/solution.py
+++ b/solution.py
@@ -91,16 +91,6 @@
         return carry
 
     lax.fori_loop(0, 16, widen, 0)
-
-    lengths.wait()
-    selected.wait()
-    names = blk[...].reshape(R * KVH, SEL)
-    total = jnp.zeros((R * KVH, T), F32)
-    for b in range(T // BLK):
-        hit = (names == me * (T // BLK) + b).astype(F32).astype(BF16)
-        spot = (iota((SEL, T), 1) // BLK == b).astype(F32).astype(BF16)
-        total = total + jnp.dot(hit, spot, preferred_element_type=F32)
-    chosen[...] = total
 
     def decode_row(r, index):
         for i in range(16):
@@ -158,6 +148,17 @@
 
     lax.fori_loop(1, N, send_query, 0)
 
+    lengths.wait()
+    selected.wait()
+    names = blk[...].reshape(R * KVH, SEL)
+    total = jnp.zeros((R * KVH, T), F32)
+    for b in range(T // BLK):
+        hit = (names == me * (T // BLK) + b).astype(F32).astype(BF16)
+        spot = (iota((SEL, T), 1) // BLK == b).astype(F32).astype(BF16)
+        total = total + jnp.dot(hit, spot, preferred_element_type=F32)
+    chosen[...] = total
+
+
     lax.fori_loop(EARLY, R // 4, decode_four, 0)
 
     whole = qbuf.at[pl.ds(0, N - 1)]
@@ -169,8 +170,8 @@
     permute = (to_row == origin).astype(F32).astype(BF16)
     for hh, (plain, turned) in enumerate(((qf0, qp0), (qf1, qp1))):
         part = qbuf[:, :, hh * HD : hh * HD + HD].reshape(N * R, HD)
-        plain[...] = part.astype(F32)
-        turned[...] = jnp.dot(part, permute, preferred_element_type=F32)
+        plain[: N * R, :] = part.astype(F32)
+        turned[: N * R, :] = jnp.dot(part, permute, preferred_element_type=F32)
 
     all_keys.wait()
     all_vals.wait()
@@ -253,7 +254,7 @@
             stat_out[p * 8 + k] = stat[pl.ds(p * 8 + k, 1), :]
 
         def send_to(k, inner):
-            to = p * 8 + k
+            to = p * 8 + lax.rem(me + 4 + k, 8)
 
             @pl.when(to != me)
             def _():
@@ -276,7 +277,7 @@
         sendbuf[block, :] = stage[block, :].astype(BF16)
 
         def send_to(k, inner):
-            to = p * 8 + k
+            to = p * 8 + lax.rem(me + 4 + k, 8)
 
             @pl.when(to != me)
             def _():
@@ -360,16 +361,16 @@
         out_specs=(vmem, vmem),
         scratch_shapes=[
             pltpu.VMEM((N, R, 2 * HD), BF16),
-            pltpu.VMEM((N * R, HD), F32),
-            pltpu.VMEM((N * R, HD), F32),
-            pltpu.VMEM((N * R, HD), F32),
-            pltpu.VMEM((N * R, HD), F32),
+            pltpu.VMEM((N * R + 16, HD), F32),
+            pltpu.VMEM((N * R + 16, HD), F32),
+            pltpu.VMEM((N * R + 16, HD), F32),
+            pltpu.VMEM((N * R + 16, HD), F32),
             pltpu.VMEM((R, T, KVH * M), jnp.int32),
             pltpu.VMEM((R, T, KVH * HD), BF16),
             pltpu.VMEM((R, T, KVH * HD), BF16),
             pltpu.VMEM((KVH * M * 8, CODES), BF16),
-            pltpu.VMEM((KVH * M * 8, 128), F32),
-            pltpu.VMEM((KVH * M * 8, 128), F32),
+            pltpu.VMEM((KVH * M * 8 + 64, 128), F32),
+            pltpu.VMEM((KVH * M * 8 + 64, 128), F32),
             pltpu.VMEM((KVH * M * 8, 128), F32),
             pltpu.VMEM((KVH * M * 8, 128), F32),
             pltpu.VMEM((R, KVH * HD, T), BF16),
@@ -383,7 +384,7 @@
             pltpu.VMEM((64, T), F32),
             pltpu.VMEM((64, T), F32),
             pltpu.VMEM((64, T), BF16),
-            pltpu.VMEM((N * 32, HD), F32),
+            pltpu.VMEM((N * 32 + 32, HD), F32),
             pltpu.VMEM((N * 32, HD), BF16),
             pltpu.VMEM((N * 32, HD), BF16),
             pltpu.VMEM((N, 128), F32),

time: 26.7 us -> 26.6 us (level)
  no operation moved by 1% of the time
where the time goes in v4:
time: 26.6 us; the launch traced here: 26.5 us
  Pallas kernels  24.7 us (93%)
  local copies, waits for them, and re-layouts  1.16 us (4%)
  between operations  0.64 us (2%)
    pallas_call x1, Pallas kernels, body(): pl.pallas_call(kernel, out_shape=(pltpu.VMEM((R, 2 * HD), BF16), pltpu.VM...  24.7 us
    unnamed x2, local copies, waits for them, and re-layouts  1.16 us

profile of v4, /device:TPU:1, one launch (start us, length us, event | category | flops | bytes accessed | tf_op | source)
XLA Modules:
  0.0 26.5 jit_solution(17687668053870706507)
XLA Ops:
  0.6 24.7 %decode_attention.1 = (bf16[16,256]{1,0:T(8,128)(2,1)S(1)}, f32[2,16]{1,0:T(2,128)S(1)}) custom-call(bf16[16,256]{1,0:T(8,128)(2,1)} %q_hbm.1, bf16[16,256,1024]{2,1,0:T(8,128)(2,1)} %k_hbm.1, bf16[16,256,1024]{2,1,0:T(8,128)(2,1)} %v_hbm.1, s32[16,256,128]{2,1,0:T(8,128)} %c_hbm.1, bf16[1024,256]{1,0:T(8,128)(2,1)} %bitcast.5, s32[16]{0:T(128)} %len_hbm.1, ...), custom_call_target="tpu_custom_call" | custom-call | tf_op jit(solution)/shard_map/decode_attention/pallas_call | solution.py:354
  25.3 0.6 %copy.11 = bf16[16,256]{1,0:T(8,128)(2,1)} copy(bf16[16,256]{1,0:T(8,128)(2,1)S(1)} %get-tuple-element.6) | data formatting | bytes 16384
  25.9 0.6 %copy.12 = f32[16,2]{0,1:T(2,128)} copy(f32[16,2]{0,1:T(2,128)S(1)} %bitcast.4) | data formatting | bytes 256

commit v5 on v4

--- a/solution.py
+++ b/solution.py
@@ -91,6 +91,14 @@
         return carry
 
     lax.fori_loop(0, 16, widen, 0)
+
+    unit = (iota((128, 128), 0) == iota((128, 128), 1)).astype(F32).astype(BF16)
+
+    def flipped(r):
+        flat = codes[r].astype(F32).astype(BF16)
+        return lax.dot_general(
+            unit, flat, (((1,), (1,)), ((), ())), preferred_element_type=F32
+        ).astype(jnp.int32)
 
     def decode_row(r, index):
         for i in range(16):
@@ -113,7 +121,7 @@
 
     two_codes(0).wait()
     two_codes(1).wait()
-    idx_a[...] = codes[0].T
+    idx_a[...] = flipped(0)
 
     def decode_four(n, carry):
         @pl.when(n < R // 4 - 1)
@@ -122,13 +130,13 @@
             two_codes(2 * n + 3).wait()
 
         r = 4 * n
-        idx_b[...] = codes[r + 1].T
+        idx_b[...] = flipped(r + 1)
         decode_row(r, idx_a)
-        idx_c[...] = codes[r + 2].T
+        idx_c[...] = flipped(r + 2)
         decode_row(r + 1, idx_b)
-        idx_d[...] = codes[r + 3].T
+        idx_d[...] = flipped(r + 3)
         decode_row(r + 2, idx_c)
-        idx_a[...] = codes[jnp.minimum(r + 4, R - 1)].T
+        idx_a[...] = flipped(jnp.minimum(r + 4, R - 1))
         decode_row(r + 3, idx_d)
         return carry
 

time: 26.6 us -> 26.6 us (level)
  no operation moved by 1% of the time
where the time goes in v5:
time: 26.6 us; the launch traced here: 26.5 us
  Pallas kernels  24.7 us (93%)
  local copies, waits for them, and re-layouts  1.16 us (4%)
  between operations  0.64 us (2%)
    pallas_call x1, Pallas kernels, body(): pl.pallas_call(kernel, out_shape=(pltpu.VMEM((R, 2 * HD), BF16), pltpu.VM...  24.7 us
    unnamed x2, local copies, waits for them, and re-layouts  1.16 us

profile of v5, /device:TPU:1, one launch (start us, length us, event | category | flops | bytes accessed | tf_op | source)
XLA Modules:
  0.0 26.5 jit_solution(8399480279615350548)
XLA Ops:
  0.6 24.7 %decode_attention.1 = (bf16[16,256]{1,0:T(8,128)(2,1)S(1)}, f32[2,16]{1,0:T(2,128)S(1)}) custom-call(bf16[16,256]{1,0:T(8,128)(2,1)} %q_hbm.1, bf16[16,256,1024]{2,1,0:T(8,128)(2,1)} %k_hbm.1, bf16[16,256,1024]{2,1,0:T(8,128)(2,1)} %v_hbm.1, s32[16,256,128]{2,1,0:T(8,128)} %c_hbm.1, bf16[1024,256]{1,0:T(8,128)(2,1)} %bitcast.5, s32[16]{0:T(128)} %len_hbm.1, ...), custom_call_target="tpu_custom_call" | custom-call | tf_op jit(solution)/shard_map/decode_attention/pallas_call | solution.py:362
  25.3 0.6 %copy.11 = bf16[16,256]{1,0:T(8,128)(2,1)} copy(bf16[16,256]{1,0:T(8,128)(2,1)S(1)} %get-tuple-element.6) | data formatting | bytes 16384
  25.9 0.6 %copy.12 = f32[16,2]{0,1:T(2,128)} copy(f32[16,2]{0,1:T(2,128)S(1)} %bitcast.4) | data formatting | bytes 256

commit v6 on v5

--- a/solution.py
+++ b/solution.py
@@ -302,6 +302,39 @@
 
         lax.fori_loop(0, 8, send_to, 0)
 
+    def send_both(n):
+        p, _ = place(n)
+        for k in range(8):
+            stat_out[p * 8 + k] = stat[pl.ds(p * 8 + k, 1), :]
+        block = pl.ds(pl.multiple_of(p * 256, 256), 256)
+        sendbuf[block, :] = stage[block, :].astype(BF16)
+
+        def send_to(k, inner):
+            to = p * 8 + lax.rem(me + 4 + k, 8)
+
+            @pl.when(to != me)
+            def _():
+                pltpu.make_async_remote_copy(
+                    src_ref=stat_out.at[to],
+                    dst_ref=stat_in.at[me],
+                    send_sem=s_send,
+                    recv_sem=s_recv,
+                    device_id={"ctx": to},
+                    device_id_type=MESH,
+                ).start()
+                pltpu.make_async_remote_copy(
+                    src_ref=sendbuf.at[pl.ds(pl.multiple_of(to * 32, 32), 32)],
+                    dst_ref=recvbuf.at[pl.ds(pl.multiple_of(me * 32, 32), 32)],
+                    send_sem=o_send,
+                    recv_sem=o_recv,
+                    device_id={"ctx": to},
+                    device_id_type=MESH,
+                ).start()
+
+            return inner
+
+        lax.fori_loop(0, 8, send_to, 0)
+
     multiply(0)
     weigh(0)
     multiply(1)
@@ -313,8 +346,7 @@
 
         @pl.when(lax.rem(n, 4) == 1)
         def _():
-            send_stats(n - 2)
-            send_values(n - 2)
+            send_both(n - 2)
 
         return carry
 

time: 26.6 us -> 26.4 us (level)
  no operation moved by 1% of the time
where the time goes in v6:
time: 26.4 us; the launch traced here: 26.3 us
  Pallas kernels  24.5 us (93%)
  local copies, waits for them, and re-layouts  1.16 us (4%)
  between operations  0.64 us (2%)
    pallas_call x1, Pallas kernels, body(): pl.pallas_call(kernel, out_shape=(pltpu.VMEM((R, 2 * HD), BF16), pltpu.VM...  24.5 us
    unnamed x2, local copies, waits for them, and re-layouts  1.16 us

profile of v6, /device:TPU:1, one launch (start us, length us, event | category | flops | bytes accessed | tf_op | source)
XLA Modules:
  0.0 26.3 jit_solution(4293563046880090606)
XLA Ops:
  0.6 24.5 %decode_attention.1 = (bf16[16,256]{1,0:T(8,128)(2,1)S(1)}, f32[2,16]{1,0:T(2,128)S(1)}) custom-call(bf16[16,256]{1,0:T(8,128)(2,1)} %q_hbm.1, bf16[16,256,1024]{2,1,0:T(8,128)(2,1)} %k_hbm.1, bf16[16,256,1024]{2,1,0:T(8,128)(2,1)} %v_hbm.1, s32[16,256,128]{2,1,0:T(8,128)} %c_hbm.1, bf16[1024,256]{1,0:T(8,128)(2,1)} %bitcast.5, s32[16]{0:T(128)} %len_hbm.1, ...), custom_call_target="tpu_custom_call" | custom-call | tf_op jit(solution)/shard_map/decode_attention/pallas_call | solution.py:394
  25.1 0.6 %copy.11 = bf16[16,256]{1,0:T(8,128)(2,1)} copy(bf16[16,256]{1,0:T(8,128)(2,1)S(1)} %get-tuple-element.6) | data formatting | bytes 16384
  25.7 0.6 %copy.12 = f32[16,2]{0,1:T(2,128)} copy(f32[16,2]{0,1:T(2,128)S(1)} %bitcast.4) | data formatting | bytes 256
